TPU v7x, 32 devices: a whole 2x2x4 slice. The times are simulated.
32 devices in a mesh: seq: 4 (over z), fft: 8 (over y, x, core).
Axes of the slice: x: 2, y: 2, z: 4, core: 2. Of those that a mesh axis runs over, the one named last changes fastest.
Arguments:
- features: bfloat16 [256, 4096], P(None, ('seq', 'fft')), may hold values from -6 to 6
- sink_order: int32 [32, 128], P(('seq', 'fft')), may hold values from 0 to 127, each once within a row
- cotangent: bfloat16 [256, 4096], P(None, ('seq', 'fft')), may hold values from -6 to 6
- w_in: bfloat16 [768, 256], replicated, may hold values from -0.375 to 0.375
- short_taps: float32 [768, 3], replicated, may hold values from -1 to 1
- w_out: bfloat16 [256, 256], replicated, may hold values from -0.375 to 0.375
- filter_one: float32 [256, 4096], P(('seq', 'fft')), may hold values from -2 to 2
- filter_two: float32 [256, 4096], P(('seq', 'fft')), may hold values from -2 to 2
Outputs:
- grad_features: bfloat16 [256, 4096], P(None, ('seq', 'fft'))
- grad_w_in: float32 [768, 256], replicated
- grad_w_out: float32 [256, 256], replicated
- grad_short: float32 [768, 3], replicated
- grad_filter_one: float32 [256, 4096], P(('seq', 'fft'))
- grad_filter_two: float32 [256, 4096], P(('seq', 'fft'))
Inputs may be any that keep to these rules, and one draw needn't show every extreme that they name: Each row of sink_order names every position of a block of 128 sinks once.
All inputs are finite; a program needn't handle non-finite values.
Results may differ from a plain program's by a relative error of at most 0.0089.
Values may be sent and summed in bfloat16 or wider, within the bound.
No kernel may reach another device: no remote copies, remote signals or barrier semaphores. Data moves between devices by JAX's collectives and lax.ppermute only.
A program may use at most 64 MiB of HBM per device.

v0:
```python
import math

import jax
import jax.numpy as jnp
from jax import lax
from jax.sharding import PartitionSpec as P

exact_mode = lax.Precision.HIGHEST
full_turn = 2.0 * math.pi


def from_behind(value, axis, steps):
    count = lax.axis_size(axis)
    first, last = (max(0, -steps), min(count, count - steps))
    return lax.ppermute(value, axis, [(source, source + steps) for source in range(first, last)])


def phase_grid(outer, inner, modulus):
    first = jnp.arange(outer, dtype=jnp.int32)[:, None]
    second = jnp.arange(inner, dtype=jnp.int32)[None, :]
    turns = first * second % modulus
    angles = turns.astype(jnp.float32) * (full_turn / modulus)
    return (jnp.cos(angles), jnp.sin(angles))


def complex_times(lower_real_part, left_imag, right_real, right_imag):
    return (
        lower_real_part * right_real - left_imag * right_imag,
        lower_real_part * right_imag + left_imag * right_real,
    )


def left_apply(table_real, table_imag, real_part, imag_part):
    form = "kn,...nm->...km"
    real_out = jnp.einsum(form, table_real, real_part, precision=exact_mode) - jnp.einsum(
        form, table_imag, imag_part, precision=exact_mode
    )
    imag_out = jnp.einsum(form, table_real, imag_part, precision=exact_mode) + jnp.einsum(
        form, table_imag, real_part, precision=exact_mode
    )
    return (real_out, imag_out)


def right_apply(real_part, imag_part, table_real, table_imag):
    form = "...n,nk->...k"
    real_out = jnp.einsum(form, real_part, table_real, precision=exact_mode) - jnp.einsum(
        form, imag_part, table_imag, precision=exact_mode
    )
    imag_out = jnp.einsum(form, imag_part, table_real, precision=exact_mode) + jnp.einsum(
        form, real_part, table_imag, precision=exact_mode
    )
    return (real_out, imag_out)


def forward_dft(real_part, imag_part):
    length = real_part.shape[-1]
    if length > 64 and length % 64 == 0:
        inner = length // 64
        leading = real_part.shape[:-1]
        real_grid = real_part.reshape(leading + (64, inner))
        imag_grid = imag_part.reshape(leading + (64, inner))
        cos_table, sin_table = phase_grid(64, 64, 64)
        real_grid, imag_grid = left_apply(cos_table, -sin_table, real_grid, imag_grid)
        twist_cos, twist_sin = phase_grid(64, inner, length)
        real_grid, imag_grid = complex_times(real_grid, imag_grid, twist_cos, -twist_sin)
        real_grid, imag_grid = forward_dft(real_grid, imag_grid)
        return (real_grid.reshape(leading + (length,)), imag_grid.reshape(leading + (length,)))
    cos_table, sin_table = phase_grid(length, length, length)
    return right_apply(real_part, imag_part, cos_table, -sin_table)


def inverse_dft(real_part, imag_part):
    length = real_part.shape[-1]
    if length > 64 and length % 64 == 0:
        inner = length // 64
        leading = real_part.shape[:-1]
        real_grid = real_part.reshape(leading + (64, inner))
        imag_grid = imag_part.reshape(leading + (64, inner))
        real_grid, imag_grid = inverse_dft(real_grid, imag_grid)
        twist_cos, twist_sin = phase_grid(64, inner, length)
        real_grid, imag_grid = complex_times(real_grid, imag_grid, twist_cos, twist_sin)
        cos_table, sin_table = phase_grid(64, 64, 64)
        real_grid, imag_grid = left_apply(cos_table, sin_table, real_grid, imag_grid)
        return (
            (real_grid / 64.0).reshape(leading + (length,)),
            (imag_grid / 64.0).reshape(leading + (length,)),
        )
    cos_table, sin_table = phase_grid(length, length, length)
    real_out, imag_out = right_apply(real_part, imag_part, cos_table, sin_table)
    return (real_out / length, imag_out / length)


def spectrum(signal):
    padded = jnp.concatenate([signal, jnp.zeros_like(signal)], axis=1)
    return forward_dft(padded, jnp.zeros_like(padded))


def to_time(spec_pair, length):
    real_out, unused = inverse_dft(spec_pair[0], spec_pair[1])
    return real_out[:, :length]


def spec_product(first, second):
    return complex_times(first[0], first[1], second[0], second[1])


def spec_conj_product(first, second):
    return complex_times(first[0], -first[1], second[0], second[1])


def local(features, sink_order, cotangent, w_in, short_taps, w_out, filter_one, filter_two):
    width = features.shape[0]
    row_count = features.shape[1]
    seq_count = lax.axis_size("seq")
    fft_count = lax.axis_size("fft")
    block_count = seq_count * fft_count
    channels = width // block_count
    length = filter_one.shape[1]
    scale = 1.0 / math.sqrt(length)
    order_local = sink_order[0]
    seq_input = jnp.take(features, order_local, axis=1)
    projected = jnp.dot(w_in, seq_input, preferred_element_type=jnp.float32)
    left_edge = from_behind(projected[:, row_count - 2 :], ("seq", "fft"), 1)
    padded_signal = jnp.concatenate([left_edge, projected], axis=1)
    mixed = short_taps[:, 0:1] * padded_signal[:, 2 : 2 + row_count]
    for offset in range(1, 3):
        mixed = (
            mixed
            + short_taps[:, offset : offset + 1]
            * padded_signal[:, 2 - offset : 2 - offset + row_count]
        )
    streams = mixed.astype(jnp.bfloat16)
    value_seq = streams[:width]
    gate_one_seq = streams[width : 2 * width]
    gate_two_seq = streams[2 * width :]
    out_grad = lax.dot_general(
        w_out, cotangent, (((0,), (0,)), ((), ())), preferred_element_type=jnp.float32
    ).astype(jnp.bfloat16)
    value_ch, gate_one_ch, gate_two_ch, out_grad_ch = (
        lax.all_to_all(
            value_seq.reshape(width, 1, row_count),
            ("seq", "fft"),
            split_axis=0,
            concat_axis=1,
            tiled=True,
        ),
        lax.all_to_all(
            gate_one_seq.reshape(width, 1, row_count),
            ("seq", "fft"),
            split_axis=0,
            concat_axis=1,
            tiled=True,
        ),
        lax.all_to_all(
            gate_two_seq.reshape(width, 1, row_count),
            ("seq", "fft"),
            split_axis=0,
            concat_axis=1,
            tiled=True,
        ),
        lax.all_to_all(
            out_grad.reshape(width, 1, row_count),
            ("seq", "fft"),
            split_axis=0,
            concat_axis=1,
            tiled=True,
        ),
    )
    value = value_ch.reshape(channels, length).astype(jnp.float32)
    gate_one = gate_one_ch.reshape(channels, length).astype(jnp.float32)
    gate_two = gate_two_ch.reshape(channels, length).astype(jnp.float32)
    out_gradf = out_grad_ch.reshape(channels, length).astype(jnp.float32)
    first_spec = spectrum(filter_one)
    second_spec = spectrum(filter_two)
    value_spec = spectrum(value)
    first_mix = to_time(spec_product(first_spec, value_spec), length)
    first_out = gate_one * first_mix
    first_out_spec = spectrum(first_out)
    second_mix = to_time(spec_product(second_spec, first_out_spec), length)
    second_out = (gate_two * second_mix).astype(jnp.bfloat16)
    grad_gate_two = (out_gradf * second_mix).astype(jnp.bfloat16)
    grad_second_mix = out_gradf * gate_two
    grad_second_spec = spectrum(grad_second_mix)
    grad_first_out = to_time(spec_conj_product(second_spec, grad_second_spec), length)
    grad_filter_two = to_time(spec_conj_product(first_out_spec, grad_second_spec), length) * scale
    grad_gate_one = (grad_first_out * first_mix).astype(jnp.bfloat16)
    grad_first_mix = grad_first_out * gate_one
    grad_first_spec = spectrum(grad_first_mix)
    grad_value = to_time(spec_conj_product(first_spec, grad_first_spec), length).astype(
        jnp.bfloat16
    )
    grad_filter_one = to_time(spec_conj_product(value_spec, grad_first_spec), length) * scale
    second_back, value_back, gate_one_back, gate_two_back = (
        lax.all_to_all(
            second_out.reshape(channels, block_count, row_count),
            ("seq", "fft"),
            split_axis=1,
            concat_axis=0,
            tiled=True,
        ),
        lax.all_to_all(
            grad_value.reshape(channels, block_count, row_count),
            ("seq", "fft"),
            split_axis=1,
            concat_axis=0,
            tiled=True,
        ),
        lax.all_to_all(
            grad_gate_one.reshape(channels, block_count, row_count),
            ("seq", "fft"),
            split_axis=1,
            concat_axis=0,
            tiled=True,
        ),
        lax.all_to_all(
            grad_gate_two.reshape(channels, block_count, row_count),
            ("seq", "fft"),
            split_axis=1,
            concat_axis=0,
            tiled=True,
        ),
    )
    second_seq = second_back.reshape(width, row_count)
    grad_streams = jnp.concatenate(
        [
            value_back.reshape(width, row_count),
            gate_one_back.reshape(width, row_count),
            gate_two_back.reshape(width, row_count),
        ],
        axis=0,
    )
    upper_boundary = from_behind(grad_streams[:, :2], ("seq", "fft"), -1)
    grad_extended = jnp.concatenate([grad_streams, upper_boundary], axis=1)
    grad_mixed = short_taps[:, 0:1] * grad_extended[:, 0:row_count]
    for offset in range(1, 3):
        grad_mixed = (
            grad_mixed
            + short_taps[:, offset : offset + 1] * grad_extended[:, offset : offset + row_count]
        )
    grad_projected = grad_mixed.astype(jnp.bfloat16)
    grad_streamsf = grad_streams.astype(jnp.float32)
    tap_terms = []
    for offset in range(3):
        tap_terms.append(
            jnp.sum(grad_streamsf * padded_signal[:, 2 - offset : 2 - offset + row_count], axis=1)
        )
    short_local = jnp.stack(tap_terms, axis=1)
    w_in_local = lax.dot_general(
        grad_projected, seq_input, (((1,), (1,)), ((), ())), preferred_element_type=jnp.float32
    )
    w_out_local = lax.dot_general(
        cotangent, second_seq, (((1,), (1,)), ((), ())), preferred_element_type=jnp.float32
    )
    w_in_total, w_out_total, short_total = lax.psum(
        (w_in_local, w_out_local, short_local), ("seq", "fft")
    )
    grad_seq = lax.dot_general(
        w_in, grad_projected, (((0,), (0,)), ((), ())), preferred_element_type=jnp.float32
    ).astype(jnp.bfloat16)
    grad_features = jnp.zeros_like(grad_seq).at[:, order_local].set(grad_seq)
    return (
        grad_features,
        w_in_total * scale,
        w_out_total * scale,
        short_total * scale,
        grad_filter_one,
        grad_filter_two,
    )


def solution(mesh):
    return jax.shard_map(
        local,
        mesh=mesh,
        in_specs=(
            P(None, ("seq", "fft")),
            P(("seq", "fft"), None),
            P(None, ("seq", "fft")),
            P(),
            P(),
            P(),
            P(("seq", "fft"), None),
            P(("seq", "fft"), None),
        ),
        out_specs=(
            P(None, ("seq", "fft")),
            P(),
            P(),
            P(),
            P(("seq", "fft"), None),
            P(("seq", "fft"), None),
        ),
        check_vma=False,
    )
```

profile of v0, /device:TPU:0, one launch (start us, length us, event | category | flops | bytes accessed | tf_op | source)
XLA Modules:
  0.0 454.2 jit_solution(16979284543562528073)
XLA Ops:
  10.2 7.3 %all-to-all-start = ((bf16[32,2,512]{2,1,0:T(2,128)(2,1)}), bf16[32,2,512]{2,1,0:T(2,128)(2,1)S(1)}, u32[]{:S(2)}, u32[]{:S(2)}) async-start(bf16[32,2,512]{2,1,0:T(2,128)(2,1)} %reshape.399), calls=%async_computation | async-start | bytes 131072 | tf_op jit(solution)/shard_map/all_to_all | solution.py:161
  19.4 2.2 collective-permute-start
  29.1 5.9 %all-to-all-start.4 = ((bf16[32,2,512]{2,1,0:T(2,128)(2,1)}), bf16[32,2,512]{2,1,0:T(2,128)(2,1)S(1)}, u32[]{:S(2)}, u32[]{:S(2)}) async-start(bf16[32,2,512]{2,1,0:T(2,128)(2,1)} %reshape.401), calls=%async_computation.4 | async-start | bytes 131072 | tf_op jit(solution)/shard_map/all_to_all | solution.py:140
  39.5 2.9 all-to-all-done.4
  42.4 3.0 all-to-all-start.1
  46.9 5.8 %all-to-all-done.1 = bf16[32,2,512]{2,1,0:T(2,128)(2,1)S(1)} async-done(((bf16[32,2,512]{2,1,0:T(2,128)(2,1)}), bf16[32,2,512]{2,1,0:T(2,128)(2,1)S(1)}, u32[]{:S(2)}, u32[]{:S(2)}) %all-to-all-start.1) | async-done | bytes 65568 | tf_op jit(solution)/shard_map/all_to_all | solution.py:154
  52.8 3.5 all-to-all-start.2
  90.9 2.2 multiply_add_fusion.15
  93.1 2.1 fusion.120
  95.2 2.1 fusion.122
  97.3 2.1 fusion.126
  99.5 3.4 convolution_add_fusion.11
  102.8 3.0 convolution_subtract_fusion.10
  105.8 2.1 fusion.108
  107.9 2.1 fusion.104
  110.0 2.2 convolution_subtract_fusion.5
  112.2 2.4 convolution_add_fusion.5
  114.5 2.1 fusion.128
  116.6 2.1 fusion.132
  118.8 2.1 convolution_subtract_fusion.11
  120.9 3.7 multiply_subtract_fusion.8
  124.6 2.2 fusion.467
  126.8 1.9 fusion.465
  128.7 2.0 convolution_subtract_fusion.4
  131.4 2.5 multiply_subtract_fusion.7
  139.8 3.3 convolution_subtract_fusion.9
  143.2 2.9 fusion.116
  152.9 2.1 fusion.98
  155.0 2.3 fusion.102
  157.4 2.2 convolution_add_fusion.3
  159.5 2.2 convolution_subtract_fusion.3
  161.8 3.9 multiply_subtract_fusion.1
  165.7 1.9 fusion.453
  167.6 2.7 fusion.451
  170.3 2.8 convolution_subtract_fusion
  176.9 3.2 convolution_add_fusion.2
  180.2 2.8 convolution_subtract_fusion.2
  184.9 1.9 fusion.480
  186.8 2.0 convolution_subtract_fusion.8
  188.8 2.5 multiply_subtract_fusion.13
  197.9 6.1 %all-to-all-start.5 = ((bf16[8,32,128]{2,0,1:T(8,128)(2,1)}), bf16[8,32,128]{2,0,1:T(8,128)(2,1)}, u32[]{:S(2)}, u32[]{:S(2)}) async-start(bf16[8,32,128]{2,0,1:T(8,128)(2,1)} %get-tuple-element.89), calls=%async_computation.5 | async-start | bytes 131072 | tf_op jit(solution)/shard_map/all_to_all | solution.py:208
  209.3 2.1 fusion.110
  211.4 2.1 fusion.114
  213.6 2.2 convolution_subtract_fusion.7
  215.8 3.9 multiply_subtract_fusion.3
  219.7 1.9 fusion.457
  223.5 2.0 convolution_subtract_fusion.1
  225.5 2.0 convolution_add_fusion.1
  227.5 1.9 fusion.471
  229.5 3.0 fusion.473
  232.5 2.0 convolution_add_fusion.6
  234.5 2.0 convolution_subtract_fusion.6
  236.6 5.1 %multiply_subtract_fusion = (f32[8,64,64,2]{2,3,1,0:T(2,128)S(1)}, f32[8,64,64,2]{2,3,1,0:T(2,128)S(1)}, f32[8,64,64,2]{2,3,1,0:T(2,128)}, f32[8,64,64,2]{2,3,1,...) fusion(f32[8,64,64,2]{2,3,1,0:T(2,128)S(1)} %copy-done.59, ...), kind=kOutput, calls=%fused_computation.139 | convolution fusion | flops 3211320 | bytes 4457472 | tf_op jit(solution)/shard_map/...n,nk->...k/dot_general | solution.py:49
  247.6 2.1 copy.358
  259.3 2.1 copy.295
  276.9 5.9 %all-to-all-start.3 = ((bf16[8,32,128]{2,0,1:T(8,128)(2,1)}), bf16[8,32,128]{2,0,1:T(8,128)(2,1)S(1)}, u32[]{:S(2)}, u32[]{:S(2)}) async-start(bf16[8,32,128]{2,0,1:T(8,128)(2,1)} %slice_bitcast_fusion.1), calls=%async_computation.3 | async-start | bytes 131072 | tf_op jit(solution)/shard_map/all_to_all | solution.py:201
  283.6 6.7 %all-to-all-done.3 = bf16[8,32,128]{2,0,1:T(8,128)(2,1)S(1)} async-done(((bf16[8,32,128]{2,0,1:T(8,128)(2,1)}), bf16[8,32,128]{2,0,1:T(8,128)(2,1)S(1)}, u32[]{:S(2)}, u32[]{:S(2)}) %all-to-all-start.3) | async-done | bytes 65568 | tf_op jit(solution)/shard_map/all_to_all | solution.py:201
  290.3 2.6 all-to-all-start.6
  293.6 6.7 %all-to-all-done.6 = bf16[8,32,128]{2,0,1:T(8,128)(2,1)S(1)} async-done(((bf16[8,32,128]{2,0,1:T(8,128)(2,1)}), bf16[8,32,128]{2,0,1:T(8,128)(2,1)S(1)}, u32[]{:S(2)}, u32[]{:S(2)}) %all-to-all-start.6) | async-done | bytes 65568 | tf_op jit(solution)/shard_map/all_to_all | solution.py:215
  300.3 2.6 all-to-all-start.7
  306.1 4.2 all-to-all-done.7
  316.1 38.8 %psum.23 = f32[768,3]{0,1:T(4,128)S(1)} all-reduce(f32[768,3]{0,1:T(4,128)S(1)} %pad_maximum_fusion.3), channel_id=1, replica_groups=mesh['seq'=4,'fft'=8] {'seq','fft'}, use_global_device_ids=true, to_apply=%region_6.7 | all-reduce | flops 2304 | bytes 18432 | tf_op jit(solution)/shard_map/psum | solution.py:254
  355.6 88.6 %all-reduce.9.cloned.1.call-done = (f32[768,256]{1,0:T(8,128)}, f32[256,256]{0,1:T(8,128)}) async-done(((f32[768,256]{1,0:T(8,128)}, f32[256,256]{0,1:T(8,128)}), (f32[768,256]{1,0:T(8,128)}, f32[256,256]{0,1:T(8,128)})) %all-reduce.9.cloned.1.call-update) | async-done | bytes 1048592 | tf_op jit(solution)/shard_map/psum | solution.py:254
  444.2 2.1 broadcast_multiply_fusion
  (334 shorter events, 128.2 us)
Async XLA Ops:
  7.2 12.0 %copy-start = (bf16[768,256]{1,0:T(8,128)(2,1)S(1)}, bf16[768,256]{1,0:T(8,128)(2,1)}, u32[]{:S(2)}) copy-start(bf16[768,256]{1,0:T(8,128)(2,1)} %param.11) | copy-start | bytes 1179652
  10.2 7.3 %copy-start.52 = (s32[1,128]{1,0:T(1,128)S(1)}, s32[1,128]{1,0:T(1,128)}, u32[]{:S(2)}) copy-start(s32[1,128]{1,0:T(1,128)} %param.9) | copy-start | bytes 1540
  10.2 7.9 %copy-start.36 = (bf16[256,128]{1,0:T(8,128)(2,1)S(1)}, bf16[256,128]{1,0:T(8,128)(2,1)}, u32[]{:S(2)}) copy-start(bf16[256,128]{1,0:T(8,128)(2,1)} %param.8) | copy-start | bytes 196612
  10.2 18.9 %all-to-all-start = ((bf16[32,2,512]{2,1,0:T(2,128)(2,1)}), bf16[32,2,512]{2,1,0:T(2,128)(2,1)S(1)}, u32[]{:S(2)}, u32[]{:S(2)}) async-start(bf16[32,2,512]{2,1,0:T(2,128)(2,1)} %reshape.399), calls=%async_computation | async-start | bytes 131072 | tf_op jit(solution)/shard_map/all_to_all | solution.py:161
  17.5 1.6 copy-start.43
  19.4 7.6 %collective-permute-start = (f32[768,2]{0,1:T(2,128)S(1)}, f32[768,2]{0,1:T(2,128)S(1)}, u32[]{:S(2)}, u32[]{:S(2)}) collective-permute-start(f32[768,2]{0,1:T(2,128)S(1)} %slice.80), channel_id=1, source_target_pairs={{0,1},{1,2},{2,3},{3,4},{4,5},{5,6},{6,7},{7,8},{8,9},{9,10},{10,1... | collective-permute-start | bytes 18440 | tf_op jit(solution)/shard_map/ppermute | solution.py:15
  22.1 0.9 copy-start.34
  23.0 0.9 copy-start.35
  29.1 13.3 %all-to-all-start.4 = ((bf16[32,2,512]{2,1,0:T(2,128)(2,1)}), bf16[32,2,512]{2,1,0:T(2,128)(2,1)S(1)}, u32[]{:S(2)}, u32[]{:S(2)}) async-start(bf16[32,2,512]{2,1,0:T(2,128)(2,1)} %reshape.401), calls=%async_computation.4 | async-start | bytes 131072 | tf_op jit(solution)/shard_map/all_to_all | solution.py:140
  39.5 16.8 %copy-start.14 = (f32[256,1,128]{2,1,0:T(1,128)}, f32[256,1,128]{2,1,0:T(1,128)S(1)}, u32[]{:S(2)}) copy-start(f32[256,1,128]{2,1,0:T(1,128)S(1)} %convert_element_type.633) | copy-start | bytes 393220
  42.4 10.4 %all-to-all-start.1 = ((bf16[32,2,512]{2,1,0:T(2,128)(2,1)}), bf16[32,2,512]{2,1,0:T(2,128)(2,1)S(1)}, u32[]{:S(2)}, u32[]{:S(2)}) async-start(bf16[32,2,512]{2,1,0:T(2,128)(2,1)} %reshape.405), calls=%async_computation.1 | async-start | bytes 131072 | tf_op jit(solution)/shard_map/all_to_all | solution.py:154
  52.8 93.3 %all-to-all-start.2 = ((bf16[32,2,512]{2,1,0:T(2,128)(2,1)}), bf16[32,2,512]{2,1,0:T(2,128)(2,1)}, u32[]{:S(2)}, u32[]{:S(2)}) async-start(bf16[32,2,512]{2,1,0:T(2,128)(2,1)} %reshape.403), calls=%async_computation.2 | async-start | bytes 131072 | tf_op jit(solution)/shard_map/all_to_all | solution.py:147
  57.0 1.0 copy-start.23
  57.0 0.9 copy-start.26
  65.0 1.5 copy-start.22
  68.8 1.0 copy-start.12
  74.3 1.5 copy-start.21
  78.1 1.0 copy-start.13
  83.9 1.5 copy-start.20
  87.6 1.0 copy-start.11
  88.7 1.5 copy-start.4
  88.7 1.5 copy-start.8
  89.4 1.1 copy-start.1
  89.4 1.3 copy-start.2
  89.4 1.4 copy-start.3
  93.1 2.1 copy-start.5
  112.1 8.8 %copy-start.53 = (f32[8,64,64,2]{2,3,1,0:T(2,128)}, f32[8,64,64,2]{2,3,1,0:T(2,128)S(1)}, u32[]{:S(2)}) copy-start(f32[8,64,64,2]{2,3,1,0:T(2,128)S(1)} %convolution_subtract_fusion.5) | copy-start | bytes 786436
  114.5 6.4 %copy-start.55 = (f32[8,64,64,2]{2,3,1,0:T(2,128)}, f32[8,64,64,2]{2,3,1,0:T(2,128)S(1)}, u32[]{:S(2)}) copy-start(f32[8,64,64,2]{2,3,1,0:T(2,128)S(1)} %convolution_add_fusion.5) | copy-start | bytes 786436
  120.9 3.7 copy-start.57
  128.7 2.0 copy-start.48
  138.8 1.0 copy-start.7
  139.0 8.0 %copy-start.24 = (f32[1,8,64,128]{3,1,2,0:T(8,128)}, f32[1,8,64,128]{3,1,2,0:T(8,128)S(1)}, u32[]{:S(2)}) copy-start(f32[1,8,64,128]{3,1,2,0:T(8,128)S(1)} %copy.557) | copy-start | bytes 786436
  157.3 4.4 copy-start.63
  157.3 4.4 copy-start.64
  159.5 2.2 copy-start.6
  159.5 2.2 copy-start.30
  159.5 2.2 copy-start.62
  186.8 2.0 copy-start.46
  186.8 2.0 copy-start.49
  196.3 0.9 copy-start.19
  196.3 1.0 copy-start.25
  197.9 79.0 %all-to-all-start.5 = ((bf16[8,32,128]{2,0,1:T(8,128)(2,1)}), bf16[8,32,128]{2,0,1:T(8,128)(2,1)}, u32[]{:S(2)}, u32[]{:S(2)}) async-start(bf16[8,32,128]{2,0,1:T(8,128)(2,1)} %get-tuple-element.89), calls=%async_computation.5 | async-start | bytes 131072 | tf_op jit(solution)/shard_map/all_to_all | solution.py:208
  211.4 4.3 copy-start.65
  213.6 2.2 copy-start.54
  213.6 2.2 copy-start.56
  213.6 2.2 copy-start.58
  232.5 4.1 copy-start.61
  234.5 2.1 copy-start.29
  234.5 2.1 copy-start.47
  234.5 2.1 copy-start.50
  234.5 2.1 copy-start.59
  234.5 2.1 copy-start.60
  252.0 1.0 copy-start.9
  253.0 1.0 copy-start.10
  275.3 0.9 copy-start.31
  276.3 6.6 %copy-start.15 = (f32[256,1,128]{2,1,0:T(1,128)S(1)}, f32[256,1,128]{2,1,0:T(1,128)}, u32[]{:S(2)}) copy-start(f32[256,1,128]{2,1,0:T(1,128)} %copy-done.14) | copy-start | bytes 393220
  276.3 6.6 %copy-start.17 = (bf16[256,1,128]{2,1,0:T(2,128)(2,1)S(1)}, bf16[256,1,128]{2,1,0:T(2,128)(2,1)}, u32[]{:S(2)}) copy-start(bf16[256,1,128]{2,1,0:T(2,128)(2,1)} %copy-done.16) | copy-start | bytes 196612
  276.9 13.4 %all-to-all-start.3 = ((bf16[8,32,128]{2,0,1:T(8,128)(2,1)}), bf16[8,32,128]{2,0,1:T(8,128)(2,1)S(1)}, u32[]{:S(2)}, u32[]{:S(2)}) async-start(bf16[8,32,128]{2,0,1:T(8,128)(2,1)} %slice_bitcast_fusion.1), calls=%async_computation.3 | async-start | bytes 131072 | tf_op jit(solution)/shard_map/all_to_all | solution.py:201
  290.3 10.0 %all-to-all-start.6 = ((bf16[8,32,128]{2,0,1:T(8,128)(2,1)}), bf16[8,32,128]{2,0,1:T(8,128)(2,1)S(1)}, u32[]{:S(2)}, u32[]{:S(2)}) async-start(bf16[8,32,128]{2,0,1:T(8,128)(2,1)} %get-tuple-element.87), calls=%async_computation.6 | async-start | bytes 131072 | tf_op jit(solution)/shard_map/all_to_all | solution.py:215
  300.3 10.0 %all-to-all-start.7 = ((bf16[8,32,128]{2,0,1:T(8,128)(2,1)}), bf16[8,32,128]{2,0,1:T(8,128)(2,1)S(1)}, u32[]{:S(2)}, u32[]{:S(2)}) async-start(bf16[8,32,128]{2,0,1:T(8,128)(2,1)} %get-tuple-element.86), calls=%async_computation.7 | async-start | bytes 131072 | tf_op jit(solution)/shard_map/all_to_all | solution.py:194
  302.8 141.3 %all-reduce.9.cloned.1.call-start = ((), (), s32[]{:S(2)}) async-start(), calls=%async_computation.8 | async-start | bytes 2097152 | tf_op jit(solution)/shard_map/psum | solution.py:254
  304.7 5.5 %copy-start.33 = (bf16[256,128]{1,0:T(8,128)(2,1)S(1)}, bf16[256,128]{1,0:T(8,128)(2,1)}, u32[]{:S(2)}) copy-start(bf16[256,128]{1,0:T(8,128)(2,1)} %param.10) | copy-start | bytes 196612
  304.8 6.4 %collective-permute-start.1 = (bf16[768,2]{0,1:T(2,128)(2,1)S(1)}, bf16[768,2]{0,1:T(2,128)(2,1)S(1)}, u32[]{:S(2)}, u32[]{:S(2)}) collective-permute-start(bf16[768,2]{0,1:T(2,128)(2,1)S(1)} %slice.90), channel_id=1, source_target_pairs={{1,0},{2,1},{3,2},{4,3},{5,4},{6,5},{7,6},{8,7},{9,8},{10,9},{11,1... | collective-permute-start | bytes 9224 | tf_op jit(solution)/shard_map/ppermute | solution.py:15
  444.2 2.1 copy-start.32
  (13 other events, 8.9 us)
Sparse Core Ops, SparseCore 0:
  314.1 130.0 all-reduce.8
where the time goes:
time: 461 us; the launch traced here: 454 us
  matrix products  179 us (39%)
  waiting for transfers between devices  115 us (25%)
  local copies, waits for them, and re-layouts  54 us (12%)
  starting transfers between devices  40.2 us (9%)
  blocking collectives  38.8 us (8%)
  between operations  16.4 us (4%)
  other arithmetic  10.9 us (2%)
    psum x1, waiting for transfers between devices, local(): lax.psum((w_in_local, w_out_local, short_local), ('seq', 'fft'))  88.6 us
    psum x1, blocking collectives, local(): lax.psum((w_in_local, w_out_local, short_local), ('seq', 'fft'))  38.8 us
    dot_general x12, matrix products, right_apply(): jnp.einsum(form, real_part, table_imag, precision=exact_mode)  36.5 us
    dot_general x12, matrix products, right_apply(): jnp.einsum(form, imag_part, table_imag, precision=exact_mode)  28.4 us
    dot_general x12, matrix products, right_apply(): jnp.einsum(form, imag_part, table_real, precision=exact_mode)  25.7 us
    dot_general x12, matrix products, right_apply(): jnp.einsum(form, real_part, table_real, precision=exact_mode)  25.7 us
    unnamed x159, local copies, waits for them, and re-layouts  18.5 us
    dot_general x18, matrix products, left_apply(): jnp.einsum(form, table_imag, real_part, precision=exact_mode)  17.5 us
  transfers between devices with their start and end apart: 11, of which 6 were waited for; matrix products, arithmetic and copies ran while one was open for 39% of the time, Pallas kernels for 0%

commit v1 on v0

v1 whole, which is shorter than its diff:
```python
import math

import jax
import jax.numpy as jnp
import numpy as np
from jax import lax
from jax.experimental import pallas as pl
from jax.experimental.pallas import tpu as pltpu
from jax.sharding import PartitionSpec as P

AXES = ("seq", "fft")
LANES = 128
bf16 = jnp.bfloat16
f32 = jnp.float32
PARAMS = pltpu.CompilerParams(vmem_limit_bytes=48 * 1024 * 1024)


def halves(table):
    high = table.astype(np.float32).astype(jnp.bfloat16)
    low = (table - high.astype(np.float64)).astype(np.float32).astype(jnp.bfloat16)
    return high, low


def make_tables(count, channels):
    length = count * LANES
    outer = np.arange(count, dtype=np.float64)
    inner = np.arange(LANES, dtype=np.float64)
    angle = 2.0 * np.pi * (outer[:, None] + 0.25) * outer[None, :] / count
    first = np.concatenate([np.cos(angle), -np.sin(angle)], axis=0)
    first = np.kron(first, np.eye(channels))
    turn = 2.0 * np.pi * (inner[:, None] * inner[None, :] % LANES) / LANES
    cos, sin = np.cos(turn), np.sin(turn)
    second = np.block([[cos, -sin], [sin, cos]])
    twist = 2.0 * np.pi * (outer[:, None] + 0.25) * inner[None, :] / length
    twist = np.repeat(twist, channels, axis=0)
    return dict(
        first=halves(first),
        first_back=halves(first.T / length),
        second=halves(second),
        second_back=halves(second.T),
        twist=(np.cos(twist).astype(np.float32), -np.sin(twist).astype(np.float32)),
    )


def split(value):
    high = value.astype(bf16)
    low = (value - high.astype(f32)).astype(bf16)
    return high, low


def dot(left, right):
    return jnp.dot(left, right, preferred_element_type=f32)


def dot_pairs(left, right):
    return dot(left[0], right[0]) + dot(left[0], right[1]) + dot(left[1], right[0])


def forward(signals, first, second, twist):
    rows = signals[0].shape[0]
    stage = dot_pairs(first, split(jnp.concatenate(signals, axis=1)))
    parts = []
    for i in range(len(signals)):
        re = stage[:rows, i * LANES : (i + 1) * LANES]
        im = stage[rows:, i * LANES : (i + 1) * LANES]
        parts.append(
            jnp.concatenate(
                [re * twist[0] - im * twist[1], re * twist[1] + im * twist[0]], axis=1
            )
        )
    spec = dot_pairs(split(jnp.concatenate(parts, axis=0)), second)
    return [
        (spec[i * rows : (i + 1) * rows, :LANES], spec[i * rows : (i + 1) * rows, LANES:])
        for i in range(len(signals))
    ]


def backward(spectra, first_back, second_back, twist):
    rows = spectra[0][0].shape[0]
    stacked = jnp.concatenate([jnp.concatenate(pair, axis=1) for pair in spectra], axis=0)
    stage = dot_pairs(split(stacked), second_back)
    parts = []
    for i in range(len(spectra)):
        re = stage[i * rows : (i + 1) * rows, :LANES]
        im = stage[i * rows : (i + 1) * rows, LANES:]
        parts.append(
            jnp.concatenate(
                [re * twist[0] + im * twist[1], im * twist[0] - re * twist[1]], axis=0
            )
        )
    out = dot_pairs(first_back, split(jnp.concatenate(parts, axis=1)))
    return [out[:, i * LANES : (i + 1) * LANES] for i in range(len(spectra))]


def times(a, b):
    return (a[0] * b[0] - a[1] * b[1], a[0] * b[1] + a[1] * b[0])


def conj_times(a, b):
    return (a[0] * b[0] + a[1] * b[1], a[0] * b[1] - a[1] * b[0])


def one_hot(order):
    size = order.shape[1]
    place = lax.broadcasted_iota(jnp.int32, (size, size), 0)
    return (place == order).astype(f32).astype(bf16)


def project_kernel(features, order, cotangent, w_in, w_out, streams_out, gather_out):
    width, row_count = features.shape
    seq_input = dot(features[...], one_hot(order[...])).astype(bf16)
    projected = dot(w_in[...], seq_input)
    out_grad = lax.dot_general(
        w_out[...], cotangent[...], (((0,), (0,)), ((), ())), preferred_element_type=f32
    )
    if len(streams_out.shape) == 3:
        blocks = streams_out.shape[0]
        parts = [projected[s * width : (s + 1) * width] for s in range(3)] + [out_grad]
        parts = [part.reshape(blocks, width // blocks, row_count) for part in parts]
        streams_out[...] = jnp.concatenate(parts, axis=1).astype(bf16)
    else:
        streams_out[: 3 * width] = projected.astype(bf16)
        streams_out[3 * width :] = out_grad.astype(bf16)
    gather_out[:width] = seq_input
    gather_out[width:] = cotangent[...]


def read_signal(ref, rows):
    if ref.shape[1] == LANES:
        return ref[...]
    return jnp.concatenate(
        [ref[:, i * LANES : (i + 1) * LANES] for i in range(ref.shape[1] // LANES)], axis=0
    )


def write_signal(ref, value):
    if ref.shape[1] == LANES:
        ref[...] = value
        return
    channels = ref.shape[0]
    for i in range(ref.shape[1] // LANES):
        ref[:, i * LANES : (i + 1) * LANES] = value[i * channels : (i + 1) * channels]


def filter_kernel(filter_one, filter_two, fh, fl, sh, sl, tr, ti, spec_one, spec_two):
    rows = spec_one.shape[0]
    signals = [read_signal(filter_one, rows), read_signal(filter_two, rows)]
    one, two = forward(
        signals, (fh[...], fl[...]), (sh[...], sl[...]), (tr[...], ti[...])
    )
    spec_one[:, :LANES] = one[0]
    spec_one[:, LANES:] = one[1]
    spec_two[:, :LANES] = two[0]
    spec_two[:, LANES:] = two[1]


def shifted(value, steps, channels):
    if steps == 0:
        return value
    rows, lanes = value.shape
    lane = lax.broadcasted_iota(jnp.int32, value.shape, 1)
    row = lax.broadcasted_iota(jnp.int32, value.shape, 0)
    turned = pltpu.roll(value, steps % lanes, 1)
    if steps > 0:
        carried = jnp.where(row < channels, 0.0, pltpu.roll(turned, channels, 0))
        return jnp.where(lane < steps, carried, turned)
    carried = jnp.where(row >= rows - channels, 0.0, pltpu.roll(turned, rows - channels, 0))
    return jnp.where(lane >= lanes + steps, carried, turned)


def mix_kernel(
    channels,
    scale,
    streams,
    taps,
    spec_one,
    spec_two,
    fh,
    fl,
    gh,
    gl,
    sh,
    sl,
    bh,
    bl,
    tr,
    ti,
    sent_out,
    short_out,
    grad_one,
    grad_two,
):
    twist = (tr[...], ti[...])
    rows = twist[0].shape[0]
    eight = taps.shape[0]
    first, second = (fh[...], fl[...]), (sh[...], sl[...])
    first_back, second_back = (gh[...], gl[...]), (bh[...], bl[...])
    if streams.shape[0] == 4 and streams.shape[1] == rows:
        pieces = [streams[s].astype(f32) for s in range(4)]
    else:
        whole = streams[...].astype(f32)
        pieces = [
            whole[:, s * channels : (s + 1) * channels].reshape(rows, LANES) for s in range(4)
        ]
    out_grad = pieces[3]

    def tap(s, k):
        column = jnp.broadcast_to(taps[:, 3 * s + k : 3 * s + k + 1], (eight, LANES))
        column = jnp.broadcast_to(column[None], (rows // eight, eight, LANES))
        return column.reshape(rows, LANES)

    late = [[shifted(pieces[s], k, channels) for k in range(3)] for s in range(3)]
    value, gate_one, gate_two = [
        sum(tap(s, k) * late[s][k] for k in range(3)) for s in range(3)
    ]
    h_one = (spec_one[:, :LANES], spec_one[:, LANES:])
    h_two = (spec_two[:, :LANES], spec_two[:, LANES:])
    value_spec, second_spec = forward([value, out_grad * gate_two], first, second, twist)
    first_mix, grad_first_out = backward(
        [times(h_one, value_spec), conj_times(h_two, second_spec)],
        first_back,
        second_back,
        twist,
    )
    first_spec, grad_first_spec = forward(
        [gate_one * first_mix, gate_one * grad_first_out], first, second, twist
    )
    second_mix, grad_value = backward(
        [times(h_two, first_spec), conj_times(h_one, grad_first_spec)],
        first_back,
        second_back,
        twist,
    )
    two, one = backward(
        [conj_times(first_spec, second_spec), conj_times(value_spec, grad_first_spec)],
        first_back,
        second_back,
        twist,
    )
    write_signal(grad_two, two * scale)
    write_signal(grad_one, one * scale)
    grads = [grad_value, grad_first_out * first_mix, out_grad * second_mix]
    sent = []
    lane = lax.broadcasted_iota(jnp.int32, (eight, LANES), 1)
    short = jnp.zeros((eight, LANES), f32)
    for s in range(3):
        sent.append(sum(tap(s, k) * shifted(grads[s], -k, channels) for k in range(3)))
        for k in range(3):
            folded = (grads[s] * late[s][k]).reshape(rows // eight, eight, LANES).sum(axis=0)
            total = jnp.sum(folded, axis=1, keepdims=True) * scale
            short = jnp.where(lane == 3 * s + k, total, short)
    sent.append(gate_two * second_mix)
    short_out[...] = short
    if len(sent_out.shape) == 3 and sent_out.shape[0] == 4 and sent_out.shape[1] == rows:
        for s in range(4):
            sent_out[s] = sent[s].astype(bf16)
    else:
        parts = [part.reshape(rows // channels, channels, LANES) for part in sent]
        sent_out[...] = jnp.concatenate(parts, axis=1).astype(bf16)


def weights_kernel(channels, scale, sent, gathered, short, out):
    blocks = sent.shape[0]
    width = gathered.shape[1] // 2
    total = jnp.zeros((4 * channels, 2 * width), f32)
    step = 2 if blocks % 2 == 0 else 1
    for i in range(0, blocks, step):
        left = jnp.concatenate([sent[i + j] for j in range(step)], axis=1)
        right = jnp.concatenate([gathered[i + j] for j in range(step)], axis=1)
        total = total + lax.dot_general(
            left, right, (((1,), (1,)), ((), ())), preferred_element_type=f32
        )
    total = total * scale
    parts = []
    for h in range(width // LANES):
        low, high = h * LANES, (h + 1) * LANES
        parts.append(total[: 3 * channels, low:high])
        parts.append(total[3 * channels :, width + low : width + high])
    parts.append(short[...])
    own = jnp.concatenate(parts, axis=0)
    own = jnp.broadcast_to(own[None], (blocks,) + own.shape)
    moved = sent[...].astype(f32)[:, : 3 * channels]
    out[...] = jnp.concatenate([moved, own], axis=1).astype(bf16)


def unorder(grad_projected, w_in, order):
    grad_seq = lax.dot_general(
        w_in, grad_projected, (((0,), (0,)), ((), ())), preferred_element_type=f32
    ).astype(bf16)
    return lax.dot_general(
        grad_seq, one_hot(order), (((1,), (1,)), ((), ())), preferred_element_type=f32
    ).astype(bf16)


def finish_kernel(channels, back, w_in, order, features_out, w_in_out, w_out_out, short_out):
    width = w_in.shape[1]
    blocks = back.shape[0]
    whole = back[...].astype(f32)

    def rows_of(start):
        return whole[:, start : start + channels].reshape(blocks * channels, LANES)

    moved = jnp.concatenate([rows_of(s * channels) for s in range(3)], axis=0).astype(bf16)
    features_out[...] = unorder(moved, w_in[...], order[...])
    for h in range(width // LANES):
        low, high = h * LANES, (h + 1) * LANES
        base = 3 * channels + 4 * channels * h
        for s in range(3):
            w_in_out[s * width : (s + 1) * width, low:high] = rows_of(base + s * channels)
        w_out_out[low:high, :] = rows_of(base + 3 * channels).T
    short = rows_of(3 * channels + 4 * channels * (width // LANES))
    for s in range(3):
        short_out[s * width : (s + 1) * width, :] = short[:, 3 * s : 3 * s + 3]


def features_kernel(moved, w_in, order, features_out):
    features_out[...] = unorder(moved[...], w_in[...], order[...])


def shape(dims, dtype=f32):
    return jax.ShapeDtypeStruct(dims, dtype)


def local(features, sink_order, cotangent, w_in, short_taps, w_out, filter_one, filter_two):
    width, row_count = features.shape
    blocks = lax.axis_size("seq") * lax.axis_size("fft")
    channels, length = filter_one.shape
    rows = channels * blocks
    scale = 1.0 / math.sqrt(length)
    whole = channels % 8 == 0
    tables = make_tables(blocks, channels)
    eight = channels if whole else 8
    mine = lax.axis_index(AXES)

    def call(kernel, outs, *args):
        return pl.pallas_call(kernel, out_shape=outs, compiler_params=PARAMS)(*args)

    dims = (blocks, 4 * channels, LANES) if whole else (4 * width, LANES)
    streams, own = call(
        project_kernel,
        (shape(dims, bf16), shape((2 * width, row_count), bf16)),
        features,
        sink_order,
        cotangent,
        w_in,
        w_out,
    )
    if not whole:
        streams = streams.reshape(4, blocks, channels, LANES).transpose(1, 0, 2, 3)
        streams = streams.reshape(blocks, 4 * channels, LANES)
    gathered = lax.all_gather(own, AXES, axis=0, tiled=False)
    arrived = lax.all_to_all(streams, AXES, split_axis=0, concat_axis=0, tiled=True)
    taps = lax.dynamic_slice_in_dim(short_taps.reshape(3, width, 3), mine * channels, channels, 1)
    taps = taps.transpose(1, 0, 2).reshape(channels, 9)
    if not whole:
        taps = jnp.tile(taps, (8 // channels, 1))
        arrived = arrived.reshape(blocks, 4, channels, LANES).transpose(1, 0, 2, 3)
        arrived = arrived.reshape(4, rows, LANES)
        filter_one, filter_two = [
            h.reshape(channels, blocks, LANES).transpose(1, 0, 2).reshape(rows, LANES)
            for h in (filter_one, filter_two)
        ]
    spec = shape((rows, 2 * LANES))
    spec_one, spec_two = call(
        filter_kernel,
        (spec, spec),
        filter_one,
        filter_two,
        *tables["first"],
        *tables["second"],
        *tables["twist"],
    )
    dims = (blocks, 4 * channels, LANES) if whole else (4, rows, LANES)
    sent, short, grad_one, grad_two = call(
        lambda *refs: mix_kernel(channels, scale, *refs),
        (
            shape(dims, bf16),
            shape((eight, LANES)),
            shape(filter_one.shape),
            shape(filter_two.shape),
        ),
        arrived,
        taps,
        spec_one,
        spec_two,
        *tables["first"],
        *tables["first_back"],
        *tables["second"],
        *tables["second_back"],
        *tables["twist"],
    )
    height = channels * (4 + 4 * (width // LANES))
    if whole:
        packed = call(
            lambda *refs: weights_kernel(channels, scale, *refs),
            shape((blocks, height, LANES), bf16),
            sent,
            gathered,
            short,
        )
        back = lax.all_to_all(packed, AXES, split_axis=0, concat_axis=0, tiled=True)
        outs = call(
            lambda *refs: finish_kernel(channels, *refs),
            (
                shape(features.shape, bf16),
                shape((3 * width, width)),
                shape((width, width)),
                shape((3 * width, 3)),
            ),
            back,
            w_in,
            sink_order,
        )
        return (*outs, grad_one, grad_two)
    sent = sent.reshape(4, blocks, channels, LANES)
    grad_in = jnp.einsum(
        "sbcp,bwp->scw", sent[:3], gathered[:, :width], preferred_element_type=f32
    )
    grad_out = jnp.einsum(
        "bcp,bwp->cw", sent[3], gathered[:, width:], preferred_element_type=f32
    )
    own = jnp.concatenate([grad_in, grad_out[None]]) * scale
    own = own.reshape(4 * channels * (width // LANES), LANES)
    short = short.reshape(8 // channels, channels, LANES).sum(axis=0)
    own = jnp.concatenate([own, short]).astype(bf16)
    moved = sent[:3].transpose(1, 0, 2, 3).reshape(blocks, 3 * channels, LANES)
    own = jnp.broadcast_to(own[None], (blocks,) + own.shape)
    packed = jnp.concatenate([moved, own], axis=1)
    back = lax.all_to_all(packed, AXES, split_axis=0, concat_axis=0, tiled=True)
    moved = back[:, : 3 * channels].reshape(blocks, 3, channels, LANES)
    moved = moved.transpose(1, 0, 2, 3).reshape(3 * width, LANES)
    weights = back[:, 3 * channels : height - channels].astype(f32)
    weights = weights.reshape(blocks, 4, channels, width).transpose(1, 0, 2, 3)
    weights = weights.reshape(4 * width, width)
    short = back[:, height - channels :, :9].astype(f32).reshape(width, 3, 3)
    short = short.transpose(1, 0, 2).reshape(3 * width, 3)
    grad_features = call(
        features_kernel, shape(features.shape, bf16), moved, w_in, sink_order
    )
    grad_one, grad_two = [
        g.reshape(blocks, channels, LANES).transpose(1, 0, 2).reshape(channels, length)
        for g in (grad_one, grad_two)
    ]
    return (
        grad_features,
        weights[: 3 * width],
        weights[3 * width :].T,
        short,
        grad_one,
        grad_two,
    )


def solution(mesh):
    columns, blocks_first, copied = P(None, AXES), P(AXES, None), P()
    return jax.shard_map(
        local,
        mesh=mesh,
        in_specs=(
            columns,
            blocks_first,
            columns,
            copied,
            copied,
            copied,
            blocks_first,
            blocks_first,
        ),
        out_specs=(columns, copied, copied, copied, blocks_first, blocks_first),
        check_vma=False,
    )
```

time: 461 us -> 115 us (0.25); the launches traced: 454 us -> 114 us
  matrix products: 179 us -> 0 us
  waiting for transfers between devices: 115 us -> 35.4 us
  starting transfers between devices: 40.2 us -> 7.34 us
  local copies, waits for them, and re-layouts: 54 us -> 23.9 us
  blocking collectives: 38.8 us -> 23.6 us
  other arithmetic: 10.9 us -> 0 us
  Pallas kernels: 0 us -> 10.1 us
    dot_general x127 -> x0, matrix products: 179 us -> none  [the longest x12 36.5 us: right_apply(): jnp.einsum(form, real_part, table_imag, precision=exact_mode)]
    psum x1 -> x0, waiting for transfers between devices: 88.6 us -> none  [local(): lax.psum((w_in_local, w_out_local, short_local), ('seq', 'fft'))]
    psum x1 -> x0, blocking collectives: 38.8 us -> none  [local(): lax.psum((w_in_local, w_out_local, short_local), ('seq', 'fft'))]
    all_gather x0 -> x1, waiting for transfers between devices: none -> 32.6 us  [local(): gathered = lax.all_gather(own, AXES, axis=0, tiled=False)]
    all_to_all x8 -> x1, starting transfers between devices: 36.8 us -> 7.3 us  [local(): lax.all_to_all(streams, AXES, split_axis=0, concat_axis=0, tiled=True)]
    all_to_all x0 -> x1, blocking collectives: none -> 23.6 us  [local(): back = lax.all_to_all(packed, AXES, split_axis=0, concat_axis=0, tiled=True)]
    all_to_all x8 -> x1, waiting for transfers between devices: 26.3 us -> 2.81 us  [local(): lax.all_to_all(streams, AXES, split_axis=0, concat_axis=0, tiled=True)]
    reshape x30 -> x2, local copies, waits for them, and re-layouts: 16.2 us -> 0.09 us  [local(): taps = taps.transpose(1, 0, 2).reshape(channels, 9)]
  transfers between devices with their start and end apart: 11 -> 2, of which waited for: 6 -> 2; matrix products, arithmetic and copies ran while one was open for 39% -> 0% of each run, Pallas kernels for 0% -> 5%
where the time goes in v1:
time: 115 us; the launch traced here: 114 us
  waiting for transfers between devices  35.4 us (31%)
  local copies, waits for them, and re-layouts  23.9 us (21%)
  blocking collectives  23.6 us (21%)
  between operations  14.1 us (12%)
  Pallas kernels  10.1 us (9%)
  starting transfers between devices  7.34 us (6%)
    all_gather x1, waiting for transfers between devices, local(): gathered = lax.all_gather(own, AXES, axis=0, tiled=False)  32.6 us
    unnamed x55, local copies, waits for them, and re-layouts  23.7 us
    all_to_all x1, blocking collectives, local(): back = lax.all_to_all(packed, AXES, split_axis=0, concat_axis=0, tiled=True)  23.6 us
    pallas_call x5, Pallas kernels, call(): return pl.pallas_call(kernel, out_shape=outs, compiler_params=PARAMS)(*args)  10.1 us
    all_to_all x1, starting transfers between devices, local(): lax.all_to_all(streams, AXES, split_axis=0, concat_axis=0, tiled=True)  7.3 us
    all_to_all x1, waiting for transfers between devices, local(): lax.all_to_all(streams, AXES, split_axis=0, concat_axis=0, tiled=True)  2.81 us
  transfers between devices with their start and end apart: 2, of which 2 were waited for; matrix products, arithmetic and copies ran while one was open for 0% of the time, Pallas kernels for 5%

profile of v1, /device:TPU:0, one launch (start us, length us, event | category | flops | bytes accessed | tf_op | source)
XLA Modules:
  0.0 114.4 jit_solution(12250256647463007290)
XLA Ops:
  7.2 0.0 copy-start
  7.2 0.0 all-gather.3.cloned.1.call-start
  7.2 0.0 copy-start.2
  7.2 1.0 copy-done.2
  8.2 0.0 copy-start.22
  8.2 0.9 copy-done.22
  9.1 0.0 copy-start.23
  9.1 0.8 copy-done.23
  10.0 0.0 copy-start.24
  10.0 0.8 copy-done.24
  10.8 0.7 copy-done.25
  11.5 1.1 %shard_map.217 = (bf16[32,32,128]{2,1,0:T(8,128)(2,1)}, bf16[512,128]{1,0:T(8,128)(2,1)}) custom-call(bf16[256,128]{1,0:T(8,128)(2,1)S(1)} %copy-done.23, s32[1,128]{1,0:T(1,128)S(1)} %copy-done.25, bf16[256,128]{1,0:T(8,128)(2,1)S(1)} %copy-done.24, bf16[768,256]{1,0:T(8,128)(2,1)S(1)} %copy-done.2, bf16[256,256]{1,0:T(8,128)(2,1)S(1)} %copy-done.22), custom_call_target="tpu_custom_call" | custom-call | tf_op jit(solution)/shard_map/pallas_call | solution.py:336
  12.6 0.0 all-gather.3.cloned.1.call-update
  12.6 7.3 %all-to-all-start = ((bf16[32,32,128]{2,1,0:T(8,128)(2,1)}), bf16[32,32,128]{2,1,0:T(8,128)(2,1)S(1)}, u32[]{:S(2)}, u32[]{:S(2)}) async-start(bf16[32,32,128]{2,1,0:T(8,128)(2,1)} %get-tuple-element.18), calls=%async_computation | async-start | bytes 524288 | tf_op jit(solution)/shard_map/all_to_all | solution.py:352
  20.0 0.0 copy-done
  20.0 0.1 dynamic-slice_bitcast_fusion
  20.1 0.1 copy.28.refs_1_
  20.1 0.9 copy-done.4
  21.1 0.0 copy-start.6
  21.1 0.9 copy-done.6
  22.0 0.0 copy-start.8
  22.0 0.9 copy-done.8
  22.9 0.0 copy-start.10
  23.0 0.9 copy-done.10
  23.9 0.0 copy-start.12
  23.9 0.9 copy-done.12
  24.8 0.0 copy-start.14
  24.8 0.9 copy-done.14
  25.7 0.9 copy-done.18
  26.6 0.0 copy-start.19
  26.6 0.9 copy-done.19
  27.5 1.0 shard_map.218
  28.5 2.8 %all-to-all-done.refs_0_ = bf16[32,32,128]{2,1,0:T(8,128)(2,1)S(1)} async-done(((bf16[32,32,128]{2,1,0:T(8,128)(2,1)}), bf16[32,32,128]{2,1,0:T(8,128)(2,1)S(1)}, u32[]{:S(2)}, u32[]{:S(2)}) %all-to-all-start) | async-done | bytes 262176 | tf_op jit(solution)/shard_map/all_to_all | solution.py:352
  31.3 0.0 copy-start.5
  31.3 0.9 copy-done.5
  32.3 0.0 copy-start.7
  32.3 0.9 copy-done.7
  33.2 0.0 copy-start.9
  33.2 0.9 copy-done.9
  34.1 0.0 copy-start.11
  34.1 0.9 copy-done.11
  35.0 0.0 copy-start.13
  35.0 0.9 copy-done.13
  35.9 0.0 copy-start.15
  35.9 0.9 copy-done.15
  36.8 0.9 copy-done.16
  37.8 0.0 copy-start.17
  37.8 0.9 copy-done.17
  38.7 0.0 copy-start.20
  38.7 0.9 copy-done.20
  39.6 0.0 copy-start.21
  39.6 0.9 copy-done.21
  40.6 0.0 copy-start.3
  40.6 0.0 copy-start.26
  40.6 5.2 %shard_map.219 = (bf16[32,32,128]{2,1,0:T(8,128)(2,1)S(1)}, f32[8,128]{1,0:T(8,128)S(1)}, f32[8,4096]{1,0:T(8,128)}, f32[8,4096]{1,0:T(8,128)}) custom-call(bf16[32,32,128]{2,1,0:T(8,128)(2,1)S(1)} %all-to-all-done.refs_0_, f32[8,9]{1,0:T(8,128)S(1)} %copy.28.refs_1_, f32[256,256]{1,0:T(8,128)S(1)} %get-tuple-element.19.refs_2_, ...), custom_call_target="tpu_custom_call" | custom-call | tf_op jit(solution)/shard_map/pallas_call | solution.py:336
  45.8 32.6 %all-gather.3.cloned.1.call-done = bf16[16384,128]{1,0:T(8,128)(2,1)} async-done(((bf16[512,128]{1,0:T(8,128)(2,1)}), bf16[16384,128]{1,0:T(8,128)(2,1)}) %all-gather.3.cloned.1.call-update) | async-done | bytes 4194320 | tf_op jit(solution)/shard_map/all_gather | solution.py:351
  78.3 0.0 copy-start.1
  78.3 2.2 %copy-done.1 = bf16[16384,128]{1,0:T(8,128)(2,1)S(1)} copy-done((bf16[16384,128]{1,0:T(8,128)(2,1)S(1)}, bf16[16384,128]{1,0:T(8,128)(2,1)}, u32[]{:S(2)}) %copy-start.1) | copy-done | bytes 4194328
  80.5 1.4 %shard_map.220 = bf16[32,96,128]{2,1,0:T(8,128)(2,1)S(1)} custom-call(bf16[32,32,128]{2,1,0:T(8,128)(2,1)S(1)} %get-tuple-element.21.refs_0_, bf16[32,512,128]{2,1,0:T(8,128)(2,1)S(1)} %bitcast.7, f32[8,128]{1,0:T(8,128)S(1)} %get-tuple-element.23.refs_2_), custom_call_target="tpu_custom_call" | custom-call | tf_op jit(solution)/shard_map/pallas_call | solution.py:336
  81.9 23.6 %all_to_all.10.refs_0_ = bf16[32,96,128]{2,1,0:T(8,128)(2,1)S(1)} all-to-all(bf16[32,96,128]{2,1,0:T(8,128)(2,1)S(1)} %shard_map.220), channel_id=1, replica_groups=mesh['seq'=4,'fft'=8] {'seq','fft'}, dimensions={0} | all-to-all | bytes 1572864 | tf_op jit(solution)/shard_map/all_to_all | solution.py:401
  105.5 0.0 copy-done.3
  105.5 0.0 copy-done.26
  105.5 1.4 %shard_map.221 = (bf16[256,128]{1,0:T(8,128)(2,1)}, f32[768,256]{1,0:T(8,128)}, f32[256,256]{1,0:T(8,128)}, f32[768,3]{1,0:T(8,128)S(1)}) custom-call(bf16[32,96,128]{2,1,0:T(8,128)(2,1)S(1)} %all_to_all.10.refs_0_, bf16[768,256]{1,0:T(8,128)(2,1)S(1)} %copy-done.3, s32[1,128]{1,0:T(1,128)S(1)} %copy-done.26), custom_call_target="tpu_custom_call" | custom-call | tf_op jit(solution)/shard_map/pallas_call | solution.py:336
  106.9 0.7 copy.29
  (5 shorter events, 0.0 us)
Async XLA Ops:
  7.2 12.8 %copy-start = (f32[768,3]{0,1:T(4,128)S(1)}, f32[768,3]{0,1:T(4,128)}, u32[]{:S(2)}) copy-start(f32[768,3]{0,1:T(4,128)} %param.22) | copy-start | bytes 27652
  7.2 71.2 %all-gather.3.cloned.1.call-start = ((), (), s32[]{:S(2)}) async-start(), calls=%async_computation.2 | async-start | bytes 4325376 | tf_op jit(solution)/shard_map/all_gather | solution.py:351
  7.2 1.0 copy-start.2
  8.2 0.9 copy-start.22
  9.1 0.8 copy-start.23
  10.0 0.8 copy-start.24
  10.8 0.7 copy-start.25
  12.6 18.7 %all-to-all-start = ((bf16[32,32,128]{2,1,0:T(8,128)(2,1)}), bf16[32,32,128]{2,1,0:T(8,128)(2,1)S(1)}, u32[]{:S(2)}, u32[]{:S(2)}) async-start(bf16[32,32,128]{2,1,0:T(8,128)(2,1)} %get-tuple-element.18), calls=%async_computation | async-start | bytes 524288 | tf_op jit(solution)/shard_map/all_to_all | solution.py:352
  20.1 1.0 copy-start.4
  21.1 0.9 copy-start.6
  22.0 0.9 copy-start.8
  22.9 0.9 copy-start.10
  23.9 0.9 copy-start.12
  24.8 0.9 copy-start.14
  25.7 0.9 copy-start.18
  26.6 0.9 copy-start.19
  31.3 1.0 copy-start.5
  32.3 1.0 copy-start.7
  33.2 0.9 copy-start.9
  34.1 0.9 copy-start.11
  35.0 0.9 copy-start.13
  35.9 0.9 copy-start.15
  36.8 0.9 copy-start.16
  37.8 0.9 copy-start.17
  38.7 0.9 copy-start.20
  39.6 0.9 copy-start.21
  40.6 64.9 %copy-start.3 = (bf16[768,256]{1,0:T(8,128)(2,1)S(1)}, bf16[768,256]{1,0:T(8,128)(2,1)}, u32[]{:S(2)}) copy-start(bf16[768,256]{1,0:T(8,128)(2,1)} %refs_1_.1) | copy-start | bytes 1179652
  40.6 64.9 %copy-start.26 = (s32[1,128]{1,0:T(1,128)S(1)}, s32[1,128]{1,0:T(1,128)}, u32[]{:S(2)}) copy-start(s32[1,128]{1,0:T(1,128)} %refs_2_.1) | copy-start | bytes 1540
  78.3 2.2 %copy-start.1 = (bf16[16384,128]{1,0:T(8,128)(2,1)S(1)}, bf16[16384,128]{1,0:T(8,128)(2,1)}, u32[]{:S(2)}) copy-start(bf16[16384,128]{1,0:T(8,128)(2,1)} %all-gather.3.cloned.1.call-done) | copy-start | bytes 12582916
Sparse Core Ops, SparseCore 0:
  12.8 65.5 all-gather.2
